TPU v7x, 32 devices: a whole 2x2x4 slice. The times are simulated.
32 devices in a mesh: req: 4 (over x, core), tp: 8 (over z, y).
Axes of the slice: x: 2, y: 2, z: 4, core: 2. Of those that a mesh axis runs over, the one named last changes fastest.
Arguments:
- hidden: bfloat16 [4, 320, 5120], P('req'), may hold values from -6 to 6
- norm_gain: float32 [5120], replicated, may hold values from 0.5 to 2
- q_weight: float32 [5120, 1024], P(('req', 'tp')), may hold values from -0.078125 to 0.078125
- k_weight: float32 [5120, 1024], P(('req', 'tp')), may hold values from -0.078125 to 0.078125
- v_weight: float32 [5120, 1024], P(('req', 'tp')), may hold values from -0.078125 to 0.078125
- o_weight: float32 [5120, 1024], P(('req', 'tp')), may hold values from -0.5 to 0.5
- key_cache: bfloat16 [4, 512, 1024], P('req', None, 'tp'), may hold values from -160 to 160
- value_cache: bfloat16 [4, 512, 1024], P('req', None, 'tp'), may hold values from -6 to 6
- text_rows: bfloat16 [4, 256, 5120], P('req', 'tp'), may hold values from -6 to 6
- text_index: int32 [4, 256], P('req'), may hold values from 0 to 511, as said below
- clip_len: int32 [4], P('req'), may hold values from 80 to 320, as said below
- text_len: int32 [4], P('req'), may hold values from 128 to 512, as said below
Outputs:
- output: bfloat16 [4, 320, 5120], P('req', 'tp')
Inputs may be any that keep to these rules, and one draw needn't show every extreme that they name: `text_index`: within a clip the entries are distinct text rows; clip 0 always recomputes rows 0 and 511. `clip_len`: some clip has exactly 320 live slots and some clip exactly 80. `text_len`: some clip has all 512 text rows live and some clip exactly 128.
All inputs are finite; a program needn't handle non-finite values.
Results may differ from a plain program's by a relative error of at most 0.012.
The roundings to bfloat16 on the way count: a program that leaves them out, or rounds other values in their place, can miss the bound.
Values may be sent and summed in bfloat16 or wider, within the bound.
A program may use at most 64 MiB of HBM per device.

v0:
```python
import math
import jax
import jax.numpy as jnp
from jax import lax
from jax.sharding import PartitionSpec as P


def on_device(
    hidden,
    norm_gain,
    q_weight,
    k_weight,
    v_weight,
    o_weight,
    key_cache,
    value_cache,
    text_rows,
    text_index,
    clip_len,
    text_len,
):
    head_width = key_cache.shape[2]
    text_total = key_cache.shape[1]
    q_half = q_weight.astype(jnp.bfloat16)
    k_half = k_weight.astype(jnp.bfloat16)
    v_half = v_weight.astype(jnp.bfloat16)
    o_half = o_weight.astype(jnp.bfloat16)
    q_block, k_block, v_block, o_block = (
        lax.all_to_all(q_half, "tp", split_axis=1, concat_axis=0, tiled=True),
        lax.all_to_all(k_half, "tp", split_axis=1, concat_axis=0, tiled=True),
        lax.all_to_all(v_half, "tp", split_axis=1, concat_axis=0, tiled=True),
        lax.all_to_all(o_half, "tp", split_axis=1, concat_axis=0, tiled=True),
    )
    q_local, k_local, v_local, o_local = (
        lax.all_gather(q_block, "req", axis=0, tiled=True),
        lax.all_gather(k_block, "req", axis=0, tiled=True),
        lax.all_gather(v_block, "req", axis=0, tiled=True),
        lax.all_gather(o_block, "req", axis=0, tiled=True),
    )
    x32 = hidden[0].astype(jnp.float32)
    mean = jnp.mean(x32, axis=-1, keepdims=True)
    centered = x32 - mean
    var = jnp.mean(centered * centered, axis=-1, keepdims=True)
    normed = (centered * lax.rsqrt(var + 1e-06) * norm_gain).astype(jnp.bfloat16)
    kv_local = jnp.concatenate([k_local, v_local], axis=1)
    new_kv = jnp.einsum(
        "crd,de->cre",
        lax.all_gather(text_rows, "tp", axis=1, tiled=True),
        kv_local,
        preferred_element_type=jnp.float32,
    ).astype(jnp.bfloat16)
    query = jnp.dot(normed, q_local, preferred_element_type=jnp.float32).astype(jnp.bfloat16)
    selector = text_index[0][None, :] == jnp.arange(text_total, dtype=jnp.int32)[:, None]
    covered = jnp.any(selector, axis=1)
    placed = jnp.dot(
        selector.astype(jnp.bfloat16), new_kv[0], preferred_element_type=jnp.float32
    ).astype(jnp.bfloat16)
    keys = jnp.where(covered[:, None], placed[:, :head_width], key_cache[0])
    values = jnp.where(covered[:, None], placed[:, head_width:], value_cache[0])
    score = lax.dot_general(
        query, keys, (((1,), (1,)), ((), ())), preferred_element_type=jnp.float32
    ) * (1.0 / math.sqrt(head_width))
    valid = jnp.arange(text_total, dtype=jnp.int32) < text_len[0]
    score = jnp.where(valid[None, :], score, -1e30)
    top = jnp.max(score, axis=-1, keepdims=True)
    expo = jnp.exp(score - top)
    weights = (expo / jnp.sum(expo, axis=-1, keepdims=True)).astype(jnp.bfloat16)
    attended = jnp.dot(weights, values, preferred_element_type=jnp.float32).astype(jnp.bfloat16)
    tp_count = lax.axis_size("tp")
    local_rows = hidden.shape[1] // tp_count
    first_row = lax.axis_index("tp") * local_rows
    summed = lax.psum_scatter(
        lax.dot_general(
            attended, o_local, (((1,), (1,)), ((), ())), preferred_element_type=jnp.float32
        ).astype(jnp.bfloat16),
        "tp",
        scatter_dimension=0,
        tiled=True,
    ).astype(jnp.float32)
    own_rows = lax.dynamic_slice_in_dim(x32, first_row, local_rows, 0)
    positions = first_row + jnp.arange(local_rows, dtype=jnp.int32)
    live = positions < clip_len[0]
    result = own_rows + jnp.where(live[:, None], summed, 0.0)
    return result.astype(jnp.bfloat16)[None]


def solution(mesh):
    return jax.shard_map(
        on_device,
        mesh=mesh,
        in_specs=(
            P("req", None, None),
            P(),
            P(("req", "tp"), None),
            P(("req", "tp"), None),
            P(("req", "tp"), None),
            P(("req", "tp"), None),
            P("req", None, "tp"),
            P("req", None, "tp"),
            P("req", "tp", None),
            P("req", None),
            P("req"),
            P("req"),
        ),
        out_specs=P("req", "tp", None),
        check_vma=False,
    )
```

profile of v0, /device:TPU:0, one launch (start us, length us, event | category | flops | bytes accessed | tf_op | source)
XLA Modules:
  0.0 247.2 jit_solution(8818809206935015885)
XLA Ops:
  6.5 0.0 all-gather.8.cloned.1.call-start
  6.5 1.1 copy_bitcast_fusion.2
  7.7 18.1 %all_to_all.76 = bf16[160,8,128]{2,0,1:T(8,128)(2,1)} all-to-all(bf16[160,8,128]{2,0,1:T(8,128)(2,1)S(1)} %copy_bitcast_fusion.2), channel_id=1, replica_groups=mesh['req'=4,'tp'=8] {'tp'}, dimensions={1} | all-to-all | bytes 655360 | tf_op jit(solution)/shard_map/all_to_all | solution.py:30
  25.8 0.0 copy-start
  25.8 0.0 all-gather.8.cloned.1.call-update
  25.8 0.0 all-gather.10.cloned.1.call-start
  25.8 1.3 copy_bitcast_fusion.1
  27.1 13.7 %all_to_all.77 = bf16[160,8,128]{2,0,1:T(8,128)(2,1)} all-to-all(bf16[160,8,128]{2,0,1:T(8,128)(2,1)S(1)} %copy_bitcast_fusion.1), channel_id=1, replica_groups=mesh['req'=4,'tp'=8] {'tp'}, dimensions={1} | all-to-all | bytes 655360 | tf_op jit(solution)/shard_map/all_to_all | solution.py:31
  40.8 0.0 all-gather.10.cloned.1.call-update
  40.9 0.0 all-gather.12.cloned.1.call-start
  40.9 0.7 all-gather.12.cloned.1.call-update
  41.6 0.0 all-gather.6.cloned.1.call-start
  41.7 1.1 copy_bitcast_fusion.3
  42.8 0.0 copy-start.3
  42.8 13.2 %all_to_all.78 = bf16[160,8,128]{2,0,1:T(8,128)(2,1)} all-to-all(bf16[160,8,128]{2,0,1:T(8,128)(2,1)S(1)} %copy_bitcast_fusion.3), channel_id=1, replica_groups=mesh['req'=4,'tp'=8] {'tp'}, dimensions={1} | all-to-all | bytes 655360 | tf_op jit(solution)/shard_map/all_to_all | solution.py:29
  56.0 0.0 all-gather.6.cloned.1.call-update
  56.1 1.9 copy_bitcast_fusion
  57.9 4.1 %all-to-all-start.3 = ((bf16[160,8,128]{2,0,1:T(8,128)(2,1)}), bf16[160,8,128]{2,0,1:T(8,128)(2,1)}, u32[]{:S(2)}, u32[]{:S(2)}) async-start(bf16[160,8,128]{2,0,1:T(8,128)(2,1)} %copy_bitcast_fusion), calls=%async_computation.3 | async-start | bytes 655360 | tf_op jit(solution)/shard_map/all_to_all | solution.py:32
  62.0 0.0 all-gather.14.cloned.1.call-start
  62.7 0.0 copy-done
  62.7 0.5 convert_reduce_fusion
  63.3 7.6 %all-to-all-done.3 = bf16[160,8,128]{2,0,1:T(8,128)(2,1)} async-done(((bf16[160,8,128]{2,0,1:T(8,128)(2,1)}), bf16[160,8,128]{2,0,1:T(8,128)(2,1)}, u32[]{:S(2)}, u32[]{:S(2)}) %all-to-all-start.3) | async-done | bytes 327712 | tf_op jit(solution)/shard_map/all_to_all | solution.py:32
  70.8 0.0 all-gather.14.cloned.1.call-update
  70.9 0.0 reduce-scatter.2.cloned.1.call-start
  70.9 0.6 iota_compare_fusion.2
  71.5 0.0 copy-done.3
  71.5 0.2 fusion.22
  71.7 1.0 multiply_reduce_fusion
  72.7 0.0 copy-start.2
  72.7 0.0 all-gather.8.cloned.1.call-done
  72.7 0.0 all-gather.10.cloned.1.call-done
  72.8 46.5 %all-gather.12.cloned.1.call-done = bf16[1,256,5120]{2,1,0:T(8,128)(2,1)} async-done(((bf16[1,32,5120]{2,1,0:T(8,128)(2,1)}), bf16[1,256,5120]{2,1,0:T(8,128)(2,1)}) %all-gather.12.cloned.1.call-update) | async-done | bytes 2621456 | tf_op jit(solution)/shard_map/all_gather | solution.py:48
  119.2 4.4 %convolution_convert_fusion.1 = bf16[512,256]{1,0:T(8,128)(2,1)} fusion(bf16[1,256,5120]{2,1,0:T(8,128)(2,1)} %all-gather.12.cloned.1.call-done, bf16[5120,128]{1,0:T(8,128)(2,1)} %all-gather.10.cloned.1.call-done, bf16[5120,128]{1,0:T(8,128)(2,1)} %all-gather.8.cloned.1.call-done, s32[256]{0:T(256)S(1)} %bitcast.84), kind=kOutput, calls=%fused_computation.16 | convolution fusion | flops 743768064 | bytes 5506048 | tf_op jit(solution)/shard_map/dot_general | solution.py:55
  123.7 0.0 copy-start.1
  123.7 13.8 %all-gather.6.cloned.1.call-done = bf16[5120,128]{1,0:T(8,128)(2,1)} async-done(((bf16[1280,128]{1,0:T(8,128)(2,1)}), bf16[5120,128]{1,0:T(8,128)(2,1)}) %all-gather.6.cloned.1.call-update) | async-done | bytes 1310736 | tf_op jit(solution)/shard_map/all_gather | solution.py:35
  137.4 0.0 copy-done.2
  137.4 3.6 %fusion.37 = (f32[320]{0:T(512)S(1)}, f32[320,512]{1,0:T(8,128)}) fusion(bf16[512,256]{1,0:T(8,128)(2,1)} %convolution_convert_fusion.1, bf16[1,512,128]{2,1,0:T(8,128)(2,1)S(1)} %copy-done.2, pred[512]{0:T(512)(128)(4,1)S(1)} %fusion.22, bf16[5120,128]{1,0:T(8,128)(2,1)} %all-gather.6.cloned.1.call-done, bf16[1,320,5120]{2,1,0:T(8,128)(2,1)S(1)} %copy-done, ...), kind=kOutput, calls=%fused_computation.50 | convolution fusion | flops 470163136 | bytes 5530368 | tf_op jit(solution)/shard_map/dot_general | solution.py:60
  141.1 1.3 fusion.21
  142.4 14.7 %all-gather.14.cloned.1.call-done = bf16[5120,128]{1,0:T(8,128)(2,1)} async-done(((bf16[1280,128]{1,0:T(8,128)(2,1)}), bf16[5120,128]{1,0:T(8,128)(2,1)}) %all-gather.14.cloned.1.call-update) | async-done | bytes 1310736 | tf_op jit(solution)/shard_map/all_gather | solution.py:38
  157.1 0.0 copy-done.1
  157.1 4.8 %convolution_convert_fusion = bf16[320,5120]{1,0:T(8,128)(2,1)} fusion(bf16[5120,128]{1,0:T(8,128)(2,1)} %all-gather.14.cloned.1.call-done, f32[320,512]{1,0:T(8,128)} %get-tuple-element.6, f32[320]{0:T(512)S(1)} %fusion.21, f32[320]{0:T(512)S(1)} %get-tuple-element.5, bf16[512,256]{1,0:T(8,128)(2,1)} %convolution_convert_fusion.1, ...), kind=kOutput, calls=%fused_computation | convolution fusion | flops 463609856 | bytes 5508096 | tf_op jit(solution)/shard_map/dot_general | solution.py:73
  161.8 0.0 reduce-scatter.2.cloned.1.call-update
  161.9 3.5 %convert_element_type.48 = f32[1,320,5120]{2,1,0:T(8,128)} convert(bf16[1,320,5120]{2,1,0:T(8,128)(2,1)S(1)} %copy-done) | non-fusion elementwise | flops 1638400 | bytes 9830400 | tf_op jit(solution)/shard_map/convert_element_type | solution.py:40
  166.0 72.1 %reduce-scatter.2.cloned.1.call-done = bf16[40,5120]{1,0:T(8,128)(2,1)} async-done(((bf16[320,5120]{1,0:T(8,128)(2,1)}), bf16[40,5120]{1,0:T(8,128)(2,1)}) %reduce-scatter.2.cloned.1.call-update) | async-done | bytes 409616 | tf_op jit(solution)/shard_map/reduce_scatter | solution.py:72
  238.1 2.2 fusion.23
  (3 shorter events, 0.0 us)
Async XLA Ops:
  6.5 66.2 %all-gather.8.cloned.1.call-start = ((), (), s32[]{:S(2)}) async-start(), calls=%async_computation.6 | async-start | bytes 1638400 | tf_op jit(solution)/shard_map/all_gather | solution.py:36
  25.8 37.0 %copy-start = (bf16[1,320,5120]{2,1,0:T(8,128)(2,1)S(1)}, bf16[1,320,5120]{2,1,0:T(8,128)(2,1)}, u32[]{:S(2)}) copy-start(bf16[1,320,5120]{2,1,0:T(8,128)(2,1)} %param.12) | copy-start | bytes 9830404
  25.8 47.0 %all-gather.10.cloned.1.call-start = ((), (), s32[]{:S(2)}) async-start(), calls=%async_computation.7 | async-start | bytes 1638400 | tf_op jit(solution)/shard_map/all_gather | solution.py:37
  40.9 78.4 %all-gather.12.cloned.1.call-start = ((), (), s32[]{:S(2)}) async-start(), calls=%async_computation.8 | async-start | bytes 2949120 | tf_op jit(solution)/shard_map/all_gather | solution.py:48
  41.6 95.8 %all-gather.6.cloned.1.call-start = ((), (), s32[]{:S(2)}) async-start(), calls=%async_computation.5 | async-start | bytes 1638400 | tf_op jit(solution)/shard_map/all_gather | solution.py:35
  42.8 28.7 %copy-start.3 = (s32[1,256]{1,0:T(1,128)S(1)}, s32[1,256]{1,0:T(1,128)}, u32[]{:S(2)}) copy-start(s32[1,256]{1,0:T(1,128)} %param.21) | copy-start | bytes 3076
  57.9 12.9 %all-to-all-start.3 = ((bf16[160,8,128]{2,0,1:T(8,128)(2,1)}), bf16[160,8,128]{2,0,1:T(8,128)(2,1)}, u32[]{:S(2)}, u32[]{:S(2)}) async-start(bf16[160,8,128]{2,0,1:T(8,128)(2,1)} %copy_bitcast_fusion), calls=%async_computation.3 | async-start | bytes 655360 | tf_op jit(solution)/shard_map/all_to_all | solution.py:32
  62.0 95.1 %all-gather.14.cloned.1.call-start = ((), (), s32[]{:S(2)}) async-start(), calls=%async_computation.9 | async-start | bytes 1638400 | tf_op jit(solution)/shard_map/all_gather | solution.py:38
  70.9 167.3 %reduce-scatter.2.cloned.1.call-start = ((), (), s32[]{:S(2)}) async-start(), calls=%async_computation.10 | async-start | bytes 3686400 | tf_op jit(solution)/shard_map/reduce_scatter | solution.py:72
  72.7 64.8 %copy-start.2 = (bf16[1,512,128]{2,1,0:T(8,128)(2,1)S(1)}, bf16[1,512,128]{2,1,0:T(8,128)(2,1)}, u32[]{:S(2)}) copy-start(bf16[1,512,128]{2,1,0:T(8,128)(2,1)} %param.18) | copy-start | bytes 393220
  123.7 33.4 %copy-start.1 = (bf16[1,512,128]{2,1,0:T(8,128)(2,1)S(1)}, bf16[1,512,128]{2,1,0:T(8,128)(2,1)}, u32[]{:S(2)}) copy-start(bf16[1,512,128]{2,1,0:T(8,128)(2,1)} %param.19) | copy-start | bytes 393220
Sparse Core Ops, SparseCore 0:
  25.9 16.5 all-gather.7
  44.1 18.1 all-gather.9
  64.5 54.6 all-gather.11
  120.6 16.7 all-gather.5
  138.9 18.1 all-gather.13
  162.0 76.1 reduce-scatter.1
where the time goes:
time: 248 us; the launch traced here: 247 us
  waiting for transfers between devices  155 us (62%)
  blocking collectives  45.1 us (18%)
  between operations  14.9 us (6%)
  other arithmetic  14.8 us (6%)
  matrix products  12.8 us (5%)
  starting transfers between devices  4.28 us (2%)
    reduce_scatter x1, waiting for transfers between devices, on_device(): lax.psum_scatter(lax.dot_general(attended, o_local, (((1,), (1,)), ((), (...  72.1 us
    all_gather x1, waiting for transfers between devices, on_device(): lax.all_gather(text_rows, 'tp', axis=1, tiled=True)  46.5 us
    all_to_all x1, blocking collectives, on_device(): lax.all_to_all(k_half, 'tp', split_axis=1, concat_axis=0, tiled=True)  18.1 us
    all_gather x1, waiting for transfers between devices, on_device(): lax.all_gather(o_block, 'req', axis=0, tiled=True)  14.7 us
    all_gather x1, waiting for transfers between devices, on_device(): lax.all_gather(q_block, 'req', axis=0, tiled=True)  13.8 us
    all_to_all x1, blocking collectives, on_device(): lax.all_to_all(v_half, 'tp', split_axis=1, concat_axis=0, tiled=True)  13.7 us
    all_to_all x1, blocking collectives, on_device(): lax.all_to_all(q_half, 'tp', split_axis=1, concat_axis=0, tiled=True)  13.2 us
    all_to_all x1, waiting for transfers between devices, on_device(): lax.all_to_all(o_half, 'tp', split_axis=1, concat_axis=0, tiled=True)  7.57 us
  transfers between devices with their start and end apart: 7, of which 5 were waited for; matrix products, arithmetic and copies ran while one was open for 8% of the time, Pallas kernels for 0%

commit v1 on v0

--- a/solution.py
+++ b/solution.py
@@ -26,7 +26,10 @@
     v_half = v_weight.astype(jnp.bfloat16)
     o_half = o_weight.astype(jnp.bfloat16)
     q_block, k_block, v_block, o_block = (
-        lax.all_to_all(q_half, "tp", split_axis=1, concat_axis=0, tiled=True),
+        jnp.concatenate(
+            lax.all_to_all(jnp.stack(jnp.split(q_half, lax.axis_size("tp"), axis=1)), "tp", 0, 0),
+            axis=0,
+        ),
         lax.all_to_all(k_half, "tp", split_axis=1, concat_axis=0, tiled=True),
         lax.all_to_all(v_half, "tp", split_axis=1, concat_axis=0, tiled=True),
         lax.all_to_all(o_half, "tp", split_axis=1, concat_axis=0, tiled=True),

time: 248 us -> 248 us (level)
  no operation moved by 1% of the time
where the time goes in v1:
time: 248 us; the launch traced here: 247 us
  waiting for transfers between devices  155 us (62%)
  blocking collectives  45.1 us (18%)
  between operations  14.9 us (6%)
  other arithmetic  14.8 us (6%)
  matrix products  12.8 us (5%)
  starting transfers between devices  4.28 us (2%)
    reduce_scatter x1, waiting for transfers between devices, on_device(): lax.psum_scatter(lax.dot_general(attended, o_local, (((1,), (1,)), ((), (...  72.1 us
    all_gather x1, waiting for transfers between devices, on_device(): lax.all_gather(text_rows, 'tp', axis=1, tiled=True)  46.2 us
    all_to_all x1, blocking collectives, on_device(): lax.all_to_all(k_half, 'tp', split_axis=1, concat_axis=0, tiled=True)  18.1 us
    all_gather x1, waiting for transfers between devices, on_device(): lax.all_gather(o_block, 'req', axis=0, tiled=True)  14.7 us
    all_gather x1, waiting for transfers between devices, on_device(): lax.all_gather(q_block, 'req', axis=0, tiled=True)  13.8 us
    all_to_all x1, blocking collectives, on_device(): lax.all_to_all(v_half, 'tp', split_axis=1, concat_axis=0, tiled=True)  13.7 us
    all_to_all x1, blocking collectives, on_device(): lax.all_to_all(jnp.stack(jnp.split(q_half, lax.axis_size('tp'), axis=1)),...  13.3 us
    all_to_all x1, waiting for transfers between devices, on_device(): lax.all_to_all(o_half, 'tp', split_axis=1, concat_axis=0, tiled=True)  7.59 us
  transfers between devices with their start and end apart: 7, of which 5 were waited for; matrix products, arithmetic and copies ran while one was open for 8% of the time, Pallas kernels for 0%

profile of v1, /device:TPU:0, one launch (start us, length us, event | category | flops | bytes accessed | tf_op | source)
XLA Modules:
  0.0 247.2 jit_solution(18000907425382071548)
XLA Ops:
  6.5 0.0 all-gather.8.cloned.1.call-start
  6.5 1.1 copy_bitcast_fusion.2
  7.7 18.1 %all_to_all.62 = bf16[160,8,128]{2,0,1:T(8,128)(2,1)} all-to-all(bf16[160,8,128]{2,0,1:T(8,128)(2,1)S(1)} %copy_bitcast_fusion.2), channel_id=1, replica_groups=mesh['req'=4,'tp'=8] {'tp'}, dimensions={1} | all-to-all | bytes 655360 | tf_op jit(solution)/shard_map/all_to_all | solution.py:33
  25.8 0.0 all-gather.8.cloned.1.call-update
  25.8 0.0 copy-start
  25.8 0.0 all-gather.10.cloned.1.call-start
  25.9 1.3 copy_bitcast_fusion.1
  27.1 13.7 %all_to_all.63 = bf16[160,8,128]{2,0,1:T(8,128)(2,1)} all-to-all(bf16[160,8,128]{2,0,1:T(8,128)(2,1)S(1)} %copy_bitcast_fusion.1), channel_id=1, replica_groups=mesh['req'=4,'tp'=8] {'tp'}, dimensions={1} | all-to-all | bytes 655360 | tf_op jit(solution)/shard_map/all_to_all | solution.py:34
  40.8 0.0 all-gather.10.cloned.1.call-update
  40.9 0.0 all-gather.12.cloned.1.call-start
  40.9 0.7 all-gather.12.cloned.1.call-update
  41.6 0.0 all-gather.6.cloned.1.call-start
  41.6 1.1 convert_element_type.51
  42.9 0.0 copy-start.3
  43.0 13.3 %all_to_all.64 = bf16[8,160,128]{2,1,0:T(8,128)(2,1)} all-to-all(bf16[8,160,128]{2,1,0:T(8,128)(2,1)S(1)} %fusion.35), channel_id=1, replica_groups=mesh['req'=4,'tp'=8] {'tp'}, dimensions={0} | all-to-all | bytes 655360 | tf_op jit(solution)/shard_map/all_to_all | solution.py:30
  56.3 0.0 all-gather.6.cloned.1.call-update
  56.3 1.9 copy_bitcast_fusion
  58.1 4.1 %all-to-all-start.3 = ((bf16[160,8,128]{2,0,1:T(8,128)(2,1)}), bf16[160,8,128]{2,0,1:T(8,128)(2,1)}, u32[]{:S(2)}, u32[]{:S(2)}) async-start(bf16[160,8,128]{2,0,1:T(8,128)(2,1)} %copy_bitcast_fusion), calls=%async_computation.3 | async-start | bytes 655360 | tf_op jit(solution)/shard_map/all_to_all | solution.py:35
  62.2 0.0 all-gather.14.cloned.1.call-start
  62.9 0.0 copy-done
  62.9 0.5 convert_reduce_fusion
  63.5 7.6 %all-to-all-done.3 = bf16[160,8,128]{2,0,1:T(8,128)(2,1)} async-done(((bf16[160,8,128]{2,0,1:T(8,128)(2,1)}), bf16[160,8,128]{2,0,1:T(8,128)(2,1)}, u32[]{:S(2)}, u32[]{:S(2)}) %all-to-all-start.3) | async-done | bytes 327712 | tf_op jit(solution)/shard_map/all_to_all | solution.py:35
  71.1 0.0 all-gather.14.cloned.1.call-update
  71.1 0.0 reduce-scatter.2.cloned.1.call-start
  71.1 0.6 iota_compare_fusion.2
  71.7 0.0 copy-done.3
  71.7 0.2 fusion.22
  71.9 1.0 multiply_reduce_fusion
  72.9 0.0 copy-start.2
  72.9 0.0 all-gather.8.cloned.1.call-done
  72.9 0.0 all-gather.10.cloned.1.call-done
  73.0 46.2 %all-gather.12.cloned.1.call-done = bf16[1,256,5120]{2,1,0:T(8,128)(2,1)} async-done(((bf16[1,32,5120]{2,1,0:T(8,128)(2,1)}), bf16[1,256,5120]{2,1,0:T(8,128)(2,1)}) %all-gather.12.cloned.1.call-update) | async-done | bytes 2621456 | tf_op jit(solution)/shard_map/all_gather | solution.py:51
  119.2 4.4 %convolution_convert_fusion.1 = bf16[512,256]{1,0:T(8,128)(2,1)} fusion(bf16[1,256,5120]{2,1,0:T(8,128)(2,1)} %all-gather.12.cloned.1.call-done, bf16[5120,128]{1,0:T(8,128)(2,1)} %all-gather.10.cloned.1.call-done, bf16[5120,128]{1,0:T(8,128)(2,1)} %all-gather.8.cloned.1.call-done, s32[256]{0:T(256)S(1)} %bitcast.109), kind=kOutput, calls=%fused_computation.16 | convolution fusion | flops 743768064 | bytes 5506048 | tf_op jit(solution)/shard_map/dot_general | solution.py:58
  123.6 0.0 copy-start.1
  123.6 13.8 %all-gather.6.cloned.1.call-done = bf16[5120,128]{1,0:T(8,128)(2,1)} async-done(((bf16[1280,128]{1,0:T(8,128)(2,1)}), bf16[5120,128]{1,0:T(8,128)(2,1)}) %all-gather.6.cloned.1.call-update) | async-done | bytes 1310736 | tf_op jit(solution)/shard_map/all_gather | solution.py:38
  137.4 0.0 copy-done.2
  137.4 3.6 %fusion.45 = (f32[320]{0:T(512)S(1)}, f32[320,512]{1,0:T(8,128)}) fusion(bf16[512,256]{1,0:T(8,128)(2,1)} %convolution_convert_fusion.1, bf16[1,512,128]{2,1,0:T(8,128)(2,1)S(1)} %copy-done.2, pred[512]{0:T(512)(128)(4,1)S(1)} %fusion.22, bf16[5120,128]{1,0:T(8,128)(2,1)} %all-gather.6.cloned.1.call-done, bf16[1,320,5120]{2,1,0:T(8,128)(2,1)S(1)} %copy-done, ...), kind=kOutput, calls=%fused_computation.64 | convolution fusion | flops 470163136 | bytes 5530368 | tf_op jit(solution)/shard_map/dot_general | solution.py:63
  141.1 1.3 fusion.21
  142.4 14.7 %all-gather.14.cloned.1.call-done = bf16[5120,128]{1,0:T(8,128)(2,1)} async-done(((bf16[1280,128]{1,0:T(8,128)(2,1)}), bf16[5120,128]{1,0:T(8,128)(2,1)}) %all-gather.14.cloned.1.call-update) | async-done | bytes 1310736 | tf_op jit(solution)/shard_map/all_gather | solution.py:41
  157.1 0.0 copy-done.1
  157.1 4.8 %convolution_convert_fusion = bf16[320,5120]{1,0:T(8,128)(2,1)} fusion(bf16[5120,128]{1,0:T(8,128)(2,1)} %all-gather.14.cloned.1.call-done, f32[320,512]{1,0:T(8,128)} %get-tuple-element.6, f32[320]{0:T(512)S(1)} %fusion.21, f32[320]{0:T(512)S(1)} %get-tuple-element.5, bf16[512,256]{1,0:T(8,128)(2,1)} %convolution_convert_fusion.1, ...), kind=kOutput, calls=%fused_computation | convolution fusion | flops 463609856 | bytes 5508096 | tf_op jit(solution)/shard_map/dot_general | solution.py:76
  161.8 0.0 reduce-scatter.2.cloned.1.call-update
  161.9 3.5 %convert_element_type.48 = f32[1,320,5120]{2,1,0:T(8,128)} convert(bf16[1,320,5120]{2,1,0:T(8,128)(2,1)S(1)} %copy-done) | non-fusion elementwise | flops 1638400 | bytes 9830400 | tf_op jit(solution)/shard_map/convert_element_type | solution.py:43
  166.0 72.1 %reduce-scatter.2.cloned.1.call-done = bf16[40,5120]{1,0:T(8,128)(2,1)} async-done(((bf16[320,5120]{1,0:T(8,128)(2,1)}), bf16[40,5120]{1,0:T(8,128)(2,1)}) %reduce-scatter.2.cloned.1.call-update) | async-done | bytes 409616 | tf_op jit(solution)/shard_map/reduce_scatter | solution.py:75
  238.1 2.2 fusion.23
  (11 shorter events, 0.2 us)
Async XLA Ops:
  6.5 66.4 %all-gather.8.cloned.1.call-start = ((), (), s32[]{:S(2)}) async-start(), calls=%async_computation.6 | async-start | bytes 1638400 | tf_op jit(solution)/shard_map/all_gather | solution.py:39
  25.8 37.1 %copy-start = (bf16[1,320,5120]{2,1,0:T(8,128)(2,1)S(1)}, bf16[1,320,5120]{2,1,0:T(8,128)(2,1)}, u32[]{:S(2)}) copy-start(bf16[1,320,5120]{2,1,0:T(8,128)(2,1)} %param.12) | copy-start | bytes 9830404
  25.8 47.2 %all-gather.10.cloned.1.call-start = ((), (), s32[]{:S(2)}) async-start(), calls=%async_computation.7 | async-start | bytes 1638400 | tf_op jit(solution)/shard_map/all_gather | solution.py:40
  40.9 78.4 %all-gather.12.cloned.1.call-start = ((), (), s32[]{:S(2)}) async-start(), calls=%async_computation.8 | async-start | bytes 2949120 | tf_op jit(solution)/shard_map/all_gather | solution.py:51
  41.6 95.8 %all-gather.6.cloned.1.call-start = ((), (), s32[]{:S(2)}) async-start(), calls=%async_computation.5 | async-start | bytes 1638400 | tf_op jit(solution)/shard_map/all_gather | solution.py:38
  42.9 28.8 %copy-start.3 = (s32[1,256]{1,0:T(1,128)S(1)}, s32[1,256]{1,0:T(1,128)}, u32[]{:S(2)}) copy-start(s32[1,256]{1,0:T(1,128)} %param.21) | copy-start | bytes 3076
  58.1 12.9 %all-to-all-start.3 = ((bf16[160,8,128]{2,0,1:T(8,128)(2,1)}), bf16[160,8,128]{2,0,1:T(8,128)(2,1)}, u32[]{:S(2)}, u32[]{:S(2)}) async-start(bf16[160,8,128]{2,0,1:T(8,128)(2,1)} %copy_bitcast_fusion), calls=%async_computation.3 | async-start | bytes 655360 | tf_op jit(solution)/shard_map/all_to_all | solution.py:35
  62.2 94.8 %all-gather.14.cloned.1.call-start = ((), (), s32[]{:S(2)}) async-start(), calls=%async_computation.9 | async-start | bytes 1638400 | tf_op jit(solution)/shard_map/all_gather | solution.py:41
  71.1 167.0 %reduce-scatter.2.cloned.1.call-start = ((), (), s32[]{:S(2)}) async-start(), calls=%async_computation.10 | async-start | bytes 3686400 | tf_op jit(solution)/shard_map/reduce_scatter | solution.py:75
  72.9 64.5 %copy-start.2 = (bf16[1,512,128]{2,1,0:T(8,128)(2,1)S(1)}, bf16[1,512,128]{2,1,0:T(8,128)(2,1)}, u32[]{:S(2)}) copy-start(bf16[1,512,128]{2,1,0:T(8,128)(2,1)} %param.18) | copy-start | bytes 393220
  123.6 33.4 %copy-start.1 = (bf16[1,512,128]{2,1,0:T(8,128)(2,1)S(1)}, bf16[1,512,128]{2,1,0:T(8,128)(2,1)}, u32[]{:S(2)}) copy-start(bf16[1,512,128]{2,1,0:T(8,128)(2,1)} %param.19) | copy-start | bytes 393220
Sparse Core Ops, SparseCore 0:
  25.9 16.5 all-gather.7
  44.1 18.1 all-gather.9
  64.5 54.6 all-gather.11
  120.6 16.7 all-gather.5
  138.8 18.1 all-gather.13
  162.0 76.1 reduce-scatter.1
